TPU v7x, 512 devices: a whole 4x4x16 slice. The times are simulated.
512 devices in a mesh: blk: 64 (over z_lo, y, x), merge: 8 (over z_hi, core).
Axes of the slice: x: 4, y: 4, z: 16 (z_hi: 4, z_lo: 4; z = z_hi * 4 + z_lo), core: 2. Of those that a mesh axis runs over, the one named last changes fastest.
Arguments:
- series: float32 [524288], P(('blk', 'merge')), may hold values from -6 to 6
- tail: float32 [63], replicated, may hold values from -6 to 6
- excl: int32 [1], replicated, may hold values from 64 to 4095
- band: int32 [1], replicated, may hold values from 12288 to 16383
Outputs:
- profile: float32 [524288], P(('blk', 'merge'))
All inputs are finite; a program needn't handle non-finite values.
Results may differ from a plain program's by a relative error of at most 0.0003.
Values sent between devices are 32-bit elements; how exact they have to be, the bound alone decides.
A program may use at most 128 MiB of HBM per device.

v0:
```python
import jax
import jax.numpy as jnp
from jax import lax
from jax.sharding import PartitionSpec as P

STEPS = 2


BIG = 4.0


def from_behind(block, axis, distance):
    devices = range(lax.axis_size(axis))
    route = [(i - distance, i) for i in devices if i - distance in devices]
    return lax.ppermute(block, axis, route)


def passed_along(block, axis, distance):
    devices = range(lax.axis_size(axis))
    route = [((i - distance) % len(devices), i) for i in devices]
    return lax.ppermute(block, axis, route)


def normalize(ext, count, width):
    windows = jnp.stack([lax.slice_in_dim(ext, k, k + count) for k in range(width)], 0)
    mean = jnp.mean(windows, 0)
    cent = windows - mean
    var = jnp.mean(cent * cent, 0)
    return cent * lax.rsqrt(var + 1e-06)


def on_device(series, tail, excl, band):
    count = series.shape[0]
    rim_len = tail.shape[0]
    width = rim_len + 1
    groups = lax.axis_size("merge")
    blocks = lax.axis_size("blk")
    rows_len = count * groups
    piece_len = 2048
    pieces_count = rows_len // piece_len
    blk_id = lax.axis_index("blk")
    grp_id = lax.axis_index("merge")
    block = lax.all_gather(series, "merge", axis=0, tiled=True)
    head = from_behind(block[:rim_len], "blk", -1)
    head = jnp.where(blk_id == blocks - 1, tail, head)
    ext = jnp.concatenate([block, head])
    row_z = normalize(ext, rows_len, width)
    own = lax.dynamic_slice_in_dim(ext, grp_id * count, count + rim_len)
    row_index = blk_id * rows_len + jnp.arange(rows_len, dtype=jnp.int32)
    col_offs = grp_id * count + jnp.arange(count, dtype=jnp.int32)
    row_parts = [jnp.full((piece_len,), BIG, jnp.float32) for part in range(pieces_count)]
    colmin = jnp.full((count,), BIG, jnp.float32)
    travel = normalize(own, count, width)
    for step in range(STEPS):
        if step > 0:
            travel, colmin = passed_along((travel, colmin), "blk", -1)
        source = (blk_id + step) % blocks
        col_index = source * rows_len + col_offs
        for part in range(pieces_count):
            lower = part * piece_len
            sub_rows = row_z[:, lower : lower + piece_len]
            sub_index = row_index[lower : lower + piece_len]
            corr = lax.dot_general(
                sub_rows,
                travel,
                (((0,), (0,)), ((), ())),
                precision=lax.Precision.HIGHEST,
                preferred_element_type=jnp.float32,
            )
            value = 1.0 - corr * (1.0 / width)
            diag = col_index[None, :] - sub_index[:, None]
            keep = (diag > excl[0]) & (diag <= band[0])
            value = jnp.where(keep, value, BIG)
            row_parts[part] = jnp.minimum(row_parts[part], jnp.min(value, 1))
            colmin = jnp.minimum(colmin, jnp.min(value, 0))
    rowmin = jnp.concatenate(row_parts)
    colmin = passed_along(colmin, "blk", STEPS - 1)
    pieces = lax.all_to_all(
        rowmin.reshape(groups, count), "merge", split_axis=0, concat_axis=0, tiled=True
    )
    mine = jnp.min(pieces, 0)
    return jnp.minimum(mine, colmin)


def solution(mesh):
    placed = (P(("blk", "merge")), P(), P(), P())
    return jax.shard_map(
        on_device, mesh=mesh, in_specs=placed, out_specs=P(("blk", "merge")), check_vma=False
    )
```

profile of v0, /device:TPU:34, one launch (start us, length us, event | category | flops | bytes accessed | tf_op | source)
XLA Modules:
  0.0 176.5 jit_solution(14914995041779323285)
XLA Ops:
  0.0 25.9 %all_gather.3 = f32[8192]{0:T(1024)S(1)} all-gather(f32[1024]{0:T(1024)} %param.4), channel_id=1, replica_groups=mesh['blk'=64,'merge'=8] {'merge'}, dimensions={0}, use_global_device_ids=true | all-gather | bytes 36864 | tf_op jit(solution)/shard_map/all_gather | solution.py:43
  25.9 2.4 %collective-permute-start = (f32[63]{0:T(128)S(1)}, f32[63]{0:T(128)S(1)}, u32[]{:S(2)}, u32[]{:S(2)}) collective-permute-start(f32[63]{0:T(128)S(1)} %slice.553), channel_id=1, source_target_pairs={{8,0},{16,8},{24,16},{32,24},{40,32},{48,40},{56,48},{64,56},{72,6... | collective-permute-start | bytes 764 | tf_op jit(solution)/shard_map/ppermute | solution.py:15
  28.4 0.6 fusion.169
  29.0 0.6 fusion.104
  30.9 0.4 collective-permute-done
  31.3 0.1 fusion.103
  31.4 0.1 add_multiply_fusion.1
  31.5 0.1 fusion.173
  31.6 0.1 fusion.172
  31.7 0.1 fusion.171
  31.8 0.1 fusion.170
  31.9 1.8 %add_multiply_fusion = (f32[8192]{0:T(1024)S(1)}, f32[8192]{0:T(1024)S(1)}, f32[8192]{0:T(1024)S(1)}, f32[8192]{0:T(1024)S(1)}, f32[8192]{0:T(1024)S(1)}, /*inde...) fusion(f32[8192]{0:T(1024)S(1)} %all_gather.3, ...), kind=kLoop, calls=%fused_computation.197 | loop fusion | flops 1040384 | bytes 2130172 | tf_op jit(solution)/shard_map/div | solution.py:26
  33.7 0.5 stack.519
  34.3 7.5 %collective-permute-start.1 = (f32[64,1024]{1,0:T(8,128)S(1)}, f32[64,1024]{1,0:T(8,128)S(1)}, u32[]{:S(2)}, u32[]{:S(2)}) collective-permute-start(f32[64,1024]{1,0:T(8,128)S(1)} %subtract_multiply_fusion.1), channel_id=1, source_target_pairs={{8,0},{16,8},{24,16},{32,24},{40,32},{48,40},{56,48},{64,56},{72,6... | collective-permute-start | bytes 786440 | tf_op jit(solution)/shard_map/ppermute | solution.py:21
  41.8 7.3 %stack.454 = f32[64,8192]{1,0:T(8,128)S(1)} concatenate(f32[1,8192]{1,0:T(1,128)S(1)} %bitcast.140, f32[1,8192]{1,0:T(1,128)} %bitcast.203, f32[1,8192]{1,0:T(1,128)} %bitcast.202, f32[1,8192]{1,0:T(1,128)} %bitcast.201, f32[1,8192]{1,0:T(1,128)} %bitcast.200, f32[1,8192]{1,0:T(1,128)} %bitcast.199, f32[1,8192]{1,0:T(1,128)} %bitcast.198, f32[1,8192]{1,0:T(1,128)} %bitcast.197, ...), dimensions={0} | concatenate | bytes 4194304 | tf_op jit(solution)/shard_map/stack | solution.py:25
  49.2 0.3 multiply_reduce_fusion
  49.5 0.2 subtract_multiply_fusion
  49.6 6.8 %fusion.30 = f32[2048,1024]{1,0:T(8,128)S(1)} fusion(f32[64,1024]{1,0:T(8,128)S(1)} %subtract_multiply_fusion.1, f32[64,8192]{1,0:T(8,128)S(1)} %subtract_multiply_fusion), kind=kOutput, calls=%fused_computation.120 | convolution fusion | flops 1610612736 | bytes 9175040 | tf_op jit(solution)/shard_map/dot_general | solution.py:63
  56.5 17.3 %fusion.34 = f32[2048,1024]{1,0:T(8,128)S(1)} fusion(f32[64,1024]{1,0:T(8,128)S(1)} %subtract_multiply_fusion.1, f32[64,8192]{1,0:T(8,128)S(1)} %subtract_multiply_fusion), kind=kOutput, calls=%fused_computation.124 | convolution fusion | flops 1610612736 | bytes 9175040 | tf_op jit(solution)/shard_map/dot_general | solution.py:63
  73.8 9.0 %fusion.38 = f32[2048,1024]{1,0:T(8,128)} fusion(f32[64,1024]{1,0:T(8,128)S(1)} %subtract_multiply_fusion.1, f32[64,8192]{1,0:T(8,128)S(1)} %subtract_multiply_fusion), kind=kOutput, calls=%fused_computation.128 | convolution fusion | flops 1610612736 | bytes 9175040 | tf_op jit(solution)/shard_map/dot_general | solution.py:63
  82.7 0.0 collective-permute-done.1
  82.7 8.9 %fusion.36 = f32[2048,1024]{1,0:T(8,128)} fusion(f32[64,1024]{1,0:T(8,128)S(1)} %collective-permute-done.1, f32[64,8192]{1,0:T(8,128)S(1)} %subtract_multiply_fusion), kind=kOutput, calls=%fused_computation.126 | convolution fusion | flops 1610612736 | bytes 9175040 | tf_op jit(solution)/shard_map/dot_general | solution.py:63
  91.7 8.9 %fusion.32 = f32[2048,1024]{1,0:T(8,128)} fusion(f32[64,1024]{1,0:T(8,128)S(1)} %collective-permute-done.1, f32[64,8192]{1,0:T(8,128)S(1)} %subtract_multiply_fusion), kind=kOutput, calls=%fused_computation.122 | convolution fusion | flops 1610612736 | bytes 9175040 | tf_op jit(solution)/shard_map/dot_general | solution.py:63
  100.6 8.9 %fusion.28 = f32[2048,1024]{1,0:T(8,128)} fusion(f32[64,1024]{1,0:T(8,128)S(1)} %collective-permute-done.1, f32[64,8192]{1,0:T(8,128)S(1)} %subtract_multiply_fusion), kind=kOutput, calls=%fused_computation.118 | convolution fusion | flops 1610612736 | bytes 9175040 | tf_op jit(solution)/shard_map/dot_general | solution.py:63
  109.5 0.0 copy-start
  109.5 0.0 copy-start.1
  109.6 0.0 copy-start.2
  109.6 0.0 copy-start.3
  109.6 9.0 %fusion.24 = f32[2048,1024]{1,0:T(8,128)} fusion(f32[64,1024]{1,0:T(8,128)S(1)} %collective-permute-done.1, f32[64,8192]{1,0:T(8,128)S(1)} %subtract_multiply_fusion), kind=kOutput, calls=%fused_computation.114 | convolution fusion | flops 1610612736 | bytes 9175040 | tf_op jit(solution)/shard_map/dot_general | solution.py:63
  118.5 0.0 copy-done
  118.5 0.0 copy-done.1
  118.5 0.0 copy-done.2
  118.5 0.0 copy-done.3
  118.6 29.8 %fusion.20 = (f32[1024]{0:T(1024)S(1)}, f32[2048]{0:T(1024)S(1)}, f32[2048]{0:T(1024)S(1)}, f32[1024]{0:T(1024)S(1)}, f32[1024]{0:T(1024)S(1)}, /*index=5*/f32[2...) fusion(s32[2048]{0:T(1024)S(1)} %get-tuple-element.118, ...), kind=kOutput, calls=%fused_computation.44 | convolution fusion | flops 1761583104 | bytes 59645960 | tf_op jit(solution)/shard_map/dot_general | solution.py:63
  148.4 7.1 %collective-permute-start.2 = (f32[1024]{0:T(1024)S(1)}, f32[1024]{0:T(1024)S(1)}, u32[]{:S(2)}, u32[]{:S(2)}) collective-permute-start(f32[1024]{0:T(1024)S(1)} %minimum_minimum_fusion.5), channel_id=1, source_target_pairs={{8,0},{16,8},{24,16},{32,24},{40,32},{48,40},{56,48},{64,56},{72,6... | collective-permute-start | bytes 12296 | tf_op jit(solution)/shard_map/ppermute | solution.py:21
  155.6 0.6 all_to_all.6
  156.2 6.6 %all-to-all-start = ((f32[8,1,1024]{2,1,0:T(1,128)}), f32[8,1,1024]{2,1,0:T(1,128)S(1)}, u32[]{:S(2)}, u32[]{:S(2)}) async-start(f32[8,1,1024]{2,1,0:T(1,128)} %all_to_all.6), calls=%async_computation | async-start | bytes 65536 | tf_op jit(solution)/shard_map/all_to_all | solution.py:78
  162.8 0.0 collective-permute-done.2
  162.8 1.9 %collective-permute-start.3 = (f32[1024]{0:T(1024)S(1)}, f32[1024]{0:T(1024)S(1)}, u32[]{:S(2)}, u32[]{:S(2)}) collective-permute-start(f32[1024]{0:T(1024)S(1)} %minimum_minimum_fusion.4), channel_id=1, source_target_pairs={{504,0},{0,8},{8,16},{16,24},{24,32},{32,40},{40,48},{48,56},{56,6... | collective-permute-start | bytes 12296 | tf_op jit(solution)/shard_map/ppermute | solution.py:21
  164.8 10.8 %all-to-all-done = f32[8,1,1024]{2,1,0:T(1,128)S(1)} async-done(((f32[8,1,1024]{2,1,0:T(1,128)}), f32[8,1,1024]{2,1,0:T(1,128)S(1)}, u32[]{:S(2)}, u32[]{:S(2)}) %all-to-all-start) | async-done | bytes 32800 | tf_op jit(solution)/shard_map/all_to_all | solution.py:78
  175.6 0.0 collective-permute-done.3
  175.6 0.6 min.67
  (19 shorter events, 0.2 us)
Async XLA Ops:
  25.9 5.4 %collective-permute-start = (f32[63]{0:T(128)S(1)}, f32[63]{0:T(128)S(1)}, u32[]{:S(2)}, u32[]{:S(2)}) collective-permute-start(f32[63]{0:T(128)S(1)} %slice.553), channel_id=1, source_target_pairs={{8,0},{16,8},{24,16},{32,24},{40,32},{48,40},{56,48},{64,56},{72,6... | collective-permute-start | bytes 764 | tf_op jit(solution)/shard_map/ppermute | solution.py:15
  34.3 48.4 %collective-permute-start.1 = (f32[64,1024]{1,0:T(8,128)S(1)}, f32[64,1024]{1,0:T(8,128)S(1)}, u32[]{:S(2)}, u32[]{:S(2)}) collective-permute-start(f32[64,1024]{1,0:T(8,128)S(1)} %subtract_multiply_fusion.1), channel_id=1, source_target_pairs={{8,0},{16,8},{24,16},{32,24},{40,32},{48,40},{56,48},{64,56},{72,6... | collective-permute-start | bytes 786440 | tf_op jit(solution)/shard_map/ppermute | solution.py:21
  109.5 9.0 %copy-start = (s32[2048]{0:T(1024)S(1)}, s32[2048]{0:T(1024)}, u32[]{:S(2)}) copy-start(s32[2048]{0:T(1024)} %get-tuple-element.119) | copy-start | bytes 24580
  109.5 9.0 %copy-start.1 = (s32[2048]{0:T(1024)S(1)}, s32[2048]{0:T(1024)}, u32[]{:S(2)}) copy-start(s32[2048]{0:T(1024)} %get-tuple-element.120) | copy-start | bytes 24580
  109.6 9.0 %copy-start.2 = (s32[1024]{0:T(1024)S(1)}, s32[1024]{0:T(1024)}, u32[]{:S(2)}) copy-start(s32[1024]{0:T(1024)} %get-tuple-element.185) | copy-start | bytes 12292
  109.6 9.0 %copy-start.3 = (s32[1024]{0:T(1024)S(1)}, s32[1024]{0:T(1024)}, u32[]{:S(2)}) copy-start(s32[1024]{0:T(1024)} %get-tuple-element.186) | copy-start | bytes 12292
  148.4 14.4 %collective-permute-start.2 = (f32[1024]{0:T(1024)S(1)}, f32[1024]{0:T(1024)S(1)}, u32[]{:S(2)}, u32[]{:S(2)}) collective-permute-start(f32[1024]{0:T(1024)S(1)} %minimum_minimum_fusion.5), channel_id=1, source_target_pairs={{8,0},{16,8},{24,16},{32,24},{40,32},{48,40},{56,48},{64,56},{72,6... | collective-permute-start | bytes 12296 | tf_op jit(solution)/shard_map/ppermute | solution.py:21
  156.2 19.4 %all-to-all-start = ((f32[8,1,1024]{2,1,0:T(1,128)}), f32[8,1,1024]{2,1,0:T(1,128)S(1)}, u32[]{:S(2)}, u32[]{:S(2)}) async-start(f32[8,1,1024]{2,1,0:T(1,128)} %all_to_all.6), calls=%async_computation | async-start | bytes 65536 | tf_op jit(solution)/shard_map/all_to_all | solution.py:78
  162.8 12.8 %collective-permute-start.3 = (f32[1024]{0:T(1024)S(1)}, f32[1024]{0:T(1024)S(1)}, u32[]{:S(2)}, u32[]{:S(2)}) collective-permute-start(f32[1024]{0:T(1024)S(1)} %minimum_minimum_fusion.4), channel_id=1, source_target_pairs={{504,0},{0,8},{8,16},{16,24},{24,32},{32,40},{40,48},{48,56},{56,6... | collective-permute-start | bytes 12296 | tf_op jit(solution)/shard_map/ppermute | solution.py:21
where the time goes:
time: 179 us; the launch traced here: 176 us
  matrix products  98.6 us (55%)
  blocking collectives  25.9 us (14%)
  starting transfers between devices  25.6 us (14%)
  waiting for transfers between devices  11.3 us (6%)
  local copies, waits for them, and re-layouts  9.4 us (5%)
  other arithmetic  3.89 us (2%)
  between operations  1.79 us (1%)
    dot_general x8, matrix products, on_device(): lax.dot_general(sub_rows, travel, (((0,), (0,)), ((), ())), precision=lax...  98.6 us
    all_gather x1, blocking collectives, on_device(): block = lax.all_gather(series, 'merge', axis=0, tiled=True)  25.9 us
    ppermute x3, starting transfers between devices, passed_along(): return lax.ppermute(block, axis, route)  16.5 us
    all_to_all x1, waiting for transfers between devices, on_device(): lax.all_to_all(rowmin.reshape(groups, count), 'merge', split_axis=0, conc...  10.8 us
    another operation x2, local copies, waits for them, and re-layouts, normalize(): jnp.stack([lax.slice_in_dim(ext, k, k + count) for k in range(width)], 0)  7.79 us
    all_to_all x1, starting transfers between devices, on_device(): lax.all_to_all(rowmin.reshape(groups, count), 'merge', split_axis=0, conc...  6.63 us
  transfers between devices with their start and end apart: 5, of which 2 were waited for; matrix products, arithmetic and copies ran while one was open for 24% of the time, Pallas kernels for 0%

commit v1 on v0

v1 whole, which is shorter than its diff:
```python
import functools

import jax
import jax.numpy as jnp
from jax import lax
from jax.experimental import pallas as pl
from jax.experimental.pallas import tpu as pltpu
from jax.sharding import PartitionSpec as P

LOW = -192.0
LANES = 128
SUBS = 8
MESH = pl.DeviceIdType.MESH


def normal_windows(line, count, width):
    length = line.shape[1]
    rows = jnp.broadcast_to(line, (SUBS, length))
    parts = [
        pltpu.roll(rows, length - (width - 1) + first, 1, stride=1, stride_axis=0)[:, :count]
        for first in range(0, width, SUBS)
    ]
    mean = jnp.sum(functools.reduce(jnp.add, parts), 0, keepdims=True) * (1.0 / width)
    cent = [part - mean for part in parts]
    squares = functools.reduce(jnp.add, [part * part for part in cent])
    var = jnp.sum(squares, 0, keepdims=True) * (1.0 / width)
    inv = lax.rsqrt(var + 1e-06)
    return jnp.concatenate([part * inv for part in cent], 0)


def halves(z):
    high = z.astype(jnp.bfloat16)
    low = (z - high.astype(jnp.float32)).astype(jnp.bfloat16)
    return high, low


def put_columns(ref, z):
    high, low = halves(z)
    width = z.shape[0]
    for at, part in enumerate((high, low, high, low)):
        ref[at * width : (at + 1) * width, :] = part


def put_rows(ref, z):
    high, low = halves(jnp.transpose(z))
    width = z.shape[0]
    ref[:, : 2 * width] = jnp.concatenate([high, high], 1)
    ref[:, 2 * width :] = jnp.concatenate([low, low], 1)


def tile(rows_ref, cols_ref, best_ref, limit_ref, base, with_columns):
    count = rows_ref.shape[0]
    step = min(256, count)
    tops = []
    for first in range(0, count, step):
        corr = jnp.dot(
            rows_ref[...], cols_ref[:, first : first + step], preferred_element_type=jnp.float32
        )
        best = None
        for lane in range(first, first + step, LANES):
            part = corr[:, lane - first : lane - first + LANES].reshape(count // SUBS, SUBS, LANES)
            limit = limit_ref[pl.ds(base - lane // SUBS, count // SUBS)]
            part = jnp.minimum(part, limit)
            if with_columns:
                tops.append(jnp.max(part, 0))
            best = part if best is None else jnp.maximum(best, part)
        best_ref[...] = jnp.maximum(best_ref[...], best.reshape(count, LANES))
    if with_columns:
        return jnp.max(jnp.concatenate(tops, 1), 0, keepdims=True)


def kernel(
    blocks, groups, width,
    series_ref, tail_ref, excl_ref, band_ref, out_ref,
    x_ref, rows_ref, own_ref, even_ref, odd_ref, best_ref, limit_ref, cols_ref, got_ref,
    send_sem, recv_sem, back_send_sem, back_recv_sem,
):
    count = series_ref.shape[1]
    unit = count // SUBS
    half = groups // 2
    blk = lax.axis_index("blk")
    grp = lax.axis_index("merge")
    rim = half + 1
    nxt = half + 2
    after = nxt + groups
    last = after + 1

    def device(d_blk, d_grp):
        return (lax.rem(blk + d_blk + blocks, blocks), lax.rem(grp + d_grp + groups, groups))

    barrier = pltpu.get_barrier_semaphore()
    sources = [device(0, t) for t in range(1, rim + 1)]
    sources += [device(1, u) for u in range(groups)]
    sources += [(lax.rem(blk + 2, blocks), 0)]
    for source in sources:
        pl.semaphore_signal(barrier, inc=1, device_id=source, device_id_type=MESH)

    x_ref[0] = series_ref[...]
    x_ref[last, :, : width - 1] = tail_ref[...]
    best_ref[...] = jnp.full(best_ref.shape, LOW, jnp.float32)

    far = 18 * unit
    base_half = far + unit
    base_own = far + 3 * unit
    excl = excl_ref[0]
    band = band_ref[0]
    skew = lax.broadcasted_iota(jnp.int32, (16, SUBS, LANES), 2)
    skew = skew - lax.broadcasted_iota(jnp.int32, (16, SUBS, LANES), 1)
    skew = skew - SUBS * lax.broadcasted_iota(jnp.int32, (16, SUBS, LANES), 0)
    sign = jnp.where(grp + half >= groups, -1, 1)

    def fill(start, stop, base, keep):
        def body(i, _):
            at = start + i * 16
            diff = skew + SUBS * (base - at)
            limit_ref[pl.ds(at, 16)] = jnp.where(keep(diff), -LOW, LOW)
            return 0

        lax.fori_loop(0, (stop - start) // 16, body, 0)

    fill(0, far, far, lambda d: (d > excl) & (d <= band))

    pl.semaphore_wait(barrier, rim + groups + jnp.where(grp == 0, groups, 0))

    def sending(src, dst, slot, target):
        return pltpu.make_async_remote_copy(
            src_ref=src, dst_ref=dst, send_sem=send_sem.at[slot], recv_sem=recv_sem.at[slot],
            device_id=target, device_id_type=MESH,
        )

    head = series_ref.at[:, :LANES]
    copies = [sending(series_ref, x_ref.at[t], t, device(0, -t)) for t in range(1, half + 1)]
    copies += [sending(head, x_ref.at[rim, :, :LANES], rim, device(0, -rim))]
    copies += [
        sending(series_ref, x_ref.at[nxt + u], nxt + u, device(-1, -u)) for u in range(groups)
    ]
    for copy in copies:
        copy.start()
    behind = lax.rem(blk + blocks - 2, blocks)

    def head_copy(u):
        return pltpu.make_async_remote_copy(
            src_ref=head, dst_ref=x_ref.at[after, :, :LANES], send_sem=send_sem.at[last + u],
            recv_sem=recv_sem.at[after], device_id=(behind, u), device_id_type=MESH,
        )

    @pl.when(grp == 0)
    def _():
        for u in range(groups):
            head_copy(u).start()

    fill(far, far + 2 * unit, base_half, lambda d: half * count + sign * d > excl)
    fill(far + 2 * unit, far + 4 * unit, base_own, lambda d: jnp.abs(d) > excl)

    for copy in copies:
        copy.wait()
    head_copy(0).wait_recv()

    @pl.when(grp == 0)
    def _():
        for u in range(groups):
            head_copy(u).wait_send()

    def windows_of_block(t):
        ends = lax.rem(grp + t, groups) == groups - 1
        over = jnp.where(blk == blocks - 1, last, nxt + lax.rem(groups - grp, groups))
        return t, jnp.where(ends, over, t + 1)

    def windows_of_next(u):
        ends = lax.rem(grp + u, groups) == groups - 1
        over = jnp.where(blk == blocks - 2, last, after)
        return nxt + u, jnp.where(ends, over, nxt + lax.rem(u + 1, groups))

    def windows(slot, rest):
        line = jnp.concatenate([x_ref[slot], x_ref[rest, :, :LANES]], 1)
        return normal_windows(line, count, width)

    near = half - 1
    pieces = near + groups

    def place(k):
        t_slot, t_rest = windows_of_block(k + 1)
        u_slot, u_rest = windows_of_next(k - near)
        inside = k < near
        return jnp.where(inside, t_slot, u_slot), jnp.where(inside, t_rest, u_rest)

    def base_of(k):
        wraps = grp + k + 1 >= groups
        t_off = jnp.where(wraps, groups, k + 1)
        u_off = groups + lax.rem(grp + k - near + groups, groups) - grp
        u_off = jnp.where(blk == blocks - 1, 17, u_off)
        return far - unit * jnp.where(k < near, t_off, u_off)

    def back(k):
        inside = k < near
        d_blk = jnp.where(inside, 0, 1)
        d_grp = jnp.where(inside, k + 1, k - near)
        return pltpu.make_async_remote_copy(
            src_ref=cols_ref.at[k], dst_ref=got_ref.at[k], send_sem=back_send_sem.at[k],
            recv_sem=back_recv_sem.at[k], device_id=device(d_blk, d_grp), device_id_type=MESH,
        )

    z = windows(*windows_of_block(0))
    put_rows(rows_ref, z)
    put_columns(own_ref, z)
    put_columns(even_ref, windows(*place(0)))

    def meet(k, now_ref):
        cols_ref[k] = tile(rows_ref, now_ref, best_ref, limit_ref, base_of(k), True)
        back(k).start()

    def pair(i, _):
        k = 2 * i
        put_columns(odd_ref, windows(*place(k + 1)))
        meet(k, even_ref)
        put_columns(even_ref, windows(*place(k + 2)))
        meet(k + 1, odd_ref)
        return 0

    lax.fori_loop(0, (pieces - 1) // 2, pair, 0)
    put_columns(odd_ref, windows(*windows_of_block(half)))
    meet(pieces - 1, even_ref)
    tile(rows_ref, odd_ref, best_ref, limit_ref, base_half, False)
    tile(rows_ref, own_ref, best_ref, limit_ref, base_own, False)
    top = jnp.max(jnp.transpose(best_ref[...]), 0, keepdims=True)
    for k in range(pieces):
        back(k).wait()
        top = jnp.maximum(top, got_ref[k])
    out_ref[...] = 1.0 - top * (1.0 / width)


def on_device(blocks, groups, series, tail, excl, band):
    count = series.shape[0]
    width = tail.shape[0] + 1
    half = groups // 2
    pieces = half - 1 + groups
    slots = half + 2 + groups + 2
    vmem = pl.BlockSpec(memory_space=pltpu.VMEM)
    smem = pl.BlockSpec(memory_space=pltpu.SMEM)
    window_cols = pltpu.VMEM((4 * width, count), jnp.bfloat16)
    out = pl.pallas_call(
        functools.partial(kernel, blocks, groups, width),
        out_shape=jax.ShapeDtypeStruct((1, count), jnp.float32),
        in_specs=[vmem, vmem, smem, smem],
        out_specs=vmem,
        scratch_shapes=[
            pltpu.VMEM((slots, 1, count), jnp.float32),
            pltpu.VMEM((count, 4 * width), jnp.bfloat16),
            window_cols,
            window_cols,
            window_cols,
            pltpu.VMEM((count, LANES), jnp.float32),
            pltpu.VMEM((22 * count // SUBS, SUBS, LANES), jnp.float32),
            pltpu.VMEM((pieces, 1, count), jnp.float32),
            pltpu.VMEM((pieces, 1, count), jnp.float32),
            pltpu.SemaphoreType.DMA((slots - 1 + groups,)),
            pltpu.SemaphoreType.DMA((slots - 1,)),
            pltpu.SemaphoreType.DMA((pieces,)),
            pltpu.SemaphoreType.DMA((pieces,)),
        ],
        compiler_params=pltpu.CompilerParams(
            collective_id=0, has_side_effects=True, vmem_limit_bytes=40 * 1024 * 1024
        ),
    )(series.reshape(1, count), tail.reshape(1, width - 1), excl, band)
    return out.reshape(count)


def solution(mesh):
    placed = (P(("blk", "merge")), P(), P(), P())
    body = functools.partial(on_device, mesh.shape["blk"], mesh.shape["merge"])
    return jax.shard_map(
        body, mesh=mesh, in_specs=placed, out_specs=P(("blk", "merge")), check_vma=False
    )
```

time: 179 us -> 49.8 us (0.28)
  the two profiles are of different devices: /device:TPU:34 before, /device:TPU:1 now
where the time goes in v1:
time: 49.8 us; the launch traced here: 49.7 us
  Pallas kernels  47.1 us (95%)
  between operations  1.34 us (3%)
  local copies, waits for them, and re-layouts  1.24 us (2%)
    pallas_call x1, Pallas kernels, on_device(): pl.pallas_call(functools.partial(kernel, blocks, groups, width), out_shap...  47.1 us
    unnamed x5, local copies, waits for them, and re-layouts  1.24 us

profile of v1, /device:TPU:1, one launch (start us, length us, event | category | flops | bytes accessed | tf_op | source)
XLA Modules:
  0.0 49.7 jit_solution(3687628519700353606)
XLA Ops:
  0.0 0.0 copy-start
  1.3 0.0 copy-start.1
  1.3 0.0 copy-done
  1.3 0.6 %copy-done.1 = f32[63]{0:T(128)S(1)} copy-done((f32[63]{0:T(128)S(1)}, f32[63]{0:T(128)}, u32[]{:S(2)}) %copy-start.1) | copy-done | bytes 276
  2.0 47.1 %shard_map.46 = f32[1,1024]{1,0:T(1,128)S(1)} custom-call(f32[1,1024]{1,0:T(1,128)S(1)} %bitcast.4, f32[1,63]{1,0:T(1,128)S(1)} %bitcast.5, s32[1]{0:T(128)S(6)} %copy.6.excl_ref, s32[1]{0:T(128)S(6)} %copy.7.band_ref), custom_call_target="tpu_custom_call" | custom-call | tf_op jit(solution)/shard_map/pallas_call | solution.py:241
  49.1 0.6 %copy.8 = f32[1024]{0:T(1024)} copy(f32[1024]{0:T(1024)S(1)} %bitcast.3) | data formatting | bytes 8192
Async XLA Ops:
  0.0 1.3 %copy-start = (f32[1024]{0:T(1024)S(1)}, f32[1024]{0:T(1024)}, u32[]{:S(2)}) copy-start(f32[1024]{0:T(1024)} %param.4) | copy-start | bytes 12292
  1.3 0.7 %copy-start.1 = (f32[63]{0:T(128)S(1)}, f32[63]{0:T(128)}, u32[]{:S(2)}) copy-start(f32[63]{0:T(128)} %param.5) | copy-start | bytes 760

commit v2 on v1

v2 whole, which is shorter than its diff:
```python
import functools

import jax
import jax.numpy as jnp
from jax import lax
from jax.experimental import pallas as pl
from jax.experimental.pallas import tpu as pltpu
from jax.sharding import PartitionSpec as P

LOW = -192.0
LANES = 128
SUBS = 8
MESH = pl.DeviceIdType.MESH


def normal_windows(line, count, width):
    length = line.shape[1]
    rows = jnp.broadcast_to(line, (SUBS, length))
    parts = [
        pltpu.roll(rows, length - (width - 1) + first, 1, stride=1, stride_axis=0)[:, :count]
        for first in range(0, width, SUBS)
    ]
    mean = jnp.sum(functools.reduce(jnp.add, parts), 0, keepdims=True) * (1.0 / width)
    cent = [part - mean for part in parts]
    squares = functools.reduce(jnp.add, [part * part for part in cent])
    var = jnp.sum(squares, 0, keepdims=True) * (1.0 / width)
    inv = lax.rsqrt(var + 1e-06)
    return jnp.concatenate([part * inv for part in cent], 0)


def halves(z):
    high = z.astype(jnp.bfloat16)
    low = (z - high.astype(jnp.float32)).astype(jnp.bfloat16)
    return high, low


def put_columns(ref, z):
    high, low = halves(z)
    width = z.shape[0]
    for at, part in enumerate((high, low, high, low)):
        ref[at * width : (at + 1) * width, :] = part


def put_rows(ref, z):
    high, low = halves(jnp.transpose(z))
    width = z.shape[0]
    ref[:, : 2 * width] = jnp.concatenate([high, high], 1)
    ref[:, 2 * width :] = jnp.concatenate([low, low], 1)


def tile(rows_ref, cols_ref, best_ref, limit_ref, row, base):
    count = cols_ref.shape[1]
    mine = pl.ds(row * count, count)
    step = min(256, count)
    tops = []
    for first in range(0, count, step):
        corr = jnp.dot(
            rows_ref[mine, :], cols_ref[:, first : first + step], preferred_element_type=jnp.float32
        )
        best = None
        for lane in range(first, first + step, LANES):
            part = corr[:, lane - first : lane - first + LANES].reshape(count // SUBS, SUBS, LANES)
            limit = limit_ref[pl.ds(base - lane // SUBS, count // SUBS)]
            part = jnp.minimum(part, limit)
            tops.append(jnp.max(part, 0))
            best = part if best is None else jnp.maximum(best, part)
        best_ref[mine, :] = jnp.maximum(best_ref[mine, :], best.reshape(count, LANES))
    return jnp.max(jnp.concatenate(tops, 1), 0, keepdims=True)


def pick(k, entries):
    out = entries[-1]
    for at in range(len(entries) - 2, -1, -1):
        out = jnp.where(k == at, entries[at], out)
    return out


SPREAD = ((0, 1, 2), (0, -1, 1), (0, 2, 3), (-1, 0, 4), (-1, -1, 5), (-1, 1, 6), (-1, 2, 7), (1, 2, 8))
PLACE = ((0, 0), (0, 1), (0, -1), (0, 2), (1, 0), (1, 1), (1, -1), (1, 2), (-1, 2))
PAIRED = 9


def kernel(
    blocks, groups, width,
    series_hbm, tail_hbm, excl_hbm, band_hbm, out_ref,
    own_ref, short_ref, tail_ref, excl_ref, band_ref, x_ref, rows_ref, even_ref, odd_ref, best_ref, limit_ref,
    cols_ref, got_ref, local_sem, send_sem, recv_sem, head_sem, back_send_sem, back_recv_sem, ready_sem,
):
    count = own_ref.shape[1]
    unit = count // SUBS
    planes = groups // 2
    blk = lax.axis_index("blk")
    grp = lax.axis_index("merge")
    plane = lax.div(grp, 2)
    core = lax.rem(grp, 2)

    def at_plane(d_plane):
        return lax.rem(plane + d_plane + 2 * planes, planes)

    def device(d_blk, d_plane, c):
        return (lax.rem(blk + d_blk + 2 * blocks, blocks), at_plane(d_plane) * 2 + c)

    sibling = device(0, 0, 1 - core)
    loads = [
        pltpu.make_async_copy(series_hbm, own_ref, local_sem.at[0]),
        pltpu.make_async_copy(tail_hbm, short_ref, local_sem.at[1]),
        pltpu.make_async_copy(excl_hbm, excl_ref, local_sem.at[2]),
        pltpu.make_async_copy(band_hbm, band_ref, local_sem.at[3]),
    ]
    for load in loads:
        load.start()

    barrier = pltpu.get_barrier_semaphore()

    def greet(target):
        pl.semaphore_signal(barrier, inc=1, device_id=target, device_id_type=MESH)

    for d_blk in (0, 1, -1):
        greet(device(d_blk, 2, 0))
    greet(sibling)
    for d_blk, d_plane in ((0, 1), (0, -1), (1, 0), (1, 1), (1, -1)):
        greet(device(d_blk, d_plane, 1))

    @pl.when(core == 1)
    def _():
        greet((lax.rem(blk + 2, blocks), jnp.where(plane == 2, 0, 1)))

        @pl.when(plane != 1)
        def _():
            greet(device(-1, -1, 1))

    loads[0].wait()
    x_ref[0, :, :count] = own_ref[...]
    first_plane = plane == 0
    far_count = 7 + jnp.where(first_plane, 1, 0)
    near_count = 11 + jnp.where(first_plane, 3, 1)
    pl.semaphore_wait(barrier, jnp.where(core == 0, far_count, near_count))
    pl.semaphore_signal(ready_sem, inc=1, device_id=sibling, device_id_type=MESH)

    def send_piece(slot, target):
        return pltpu.make_async_remote_copy(
            src_ref=own_ref, dst_ref=x_ref.at[slot, :, :count], send_sem=send_sem.at[slot],
            recv_sem=recv_sem.at[slot], device_id=target, device_id_type=MESH,
        )

    def send_head(slot, at, target):
        return pltpu.make_async_remote_copy(
            src_ref=own_ref.at[:, :LANES], dst_ref=x_ref.at[slot, :, count:], send_sem=send_sem.at[10 + at],
            recv_sem=head_sem.at[0 if at in (0, 9) else at], device_id=target, device_id_type=MESH,
        )

    back_blk = jnp.where(first_plane, -1, 0)
    pieces = {slot: send_piece(slot, device(d, dp, core)) for d, dp, slot in SPREAD}
    pieces[PAIRED] = send_piece(PAIRED, sibling)
    heads_odd = {slot: send_head(slot, slot, device(d, dp, 0)) for d, dp, slot in SPREAD}
    heads_even = {slot: send_head(slot, slot, device(back_blk + d, dp - 1, 1)) for d, dp, slot in SPREAD}
    heads_even[0] = send_head(0, 0, device(back_blk, -1, 1))
    heads_even[9] = send_head(PAIRED, 9, device(back_blk, -1, 0))

    @pl.when(core == 0)
    def _():
        for slot in (3, 7, 8):
            pieces[slot].start()
        for slot in (1, 5):
            heads_even[slot].start()
        pl.semaphore_wait(ready_sem, 1)
        pieces[PAIRED].start()
        for slot in (0, 9, 2, 3, 4, 6, 7, 8):
            heads_even[slot].start()
        for slot in (1, 2, 5, 6, 4):
            pieces[slot].start()

    @pl.when(core == 1)
    def _():
        pieces[PAIRED].start()
        for slot in (1, 2, 5, 6, 4):
            pieces[slot].start()
        for slot in (1, 2, 5, 6, 4):
            heads_odd[slot].start()
        pl.semaphore_wait(ready_sem, 1)
        for slot in (3, 7, 8):
            pieces[slot].start()
        for slot in (3, 7, 8):
            heads_odd[slot].start()

    for load in loads[1:]:
        load.wait()
    tail_ref[...] = jnp.zeros(tail_ref.shape, jnp.float32)
    tail_ref[:, : width - 1] = short_ref[...]
    best_ref[...] = jnp.full(best_ref.shape, LOW, jnp.float32)

    far = 18 * unit
    base_own = 37 * unit
    total = 38 * unit
    excl = excl_ref[0]
    band = band_ref[0]
    skew = lax.broadcasted_iota(jnp.int32, (16, SUBS, LANES), 2)
    skew = skew - lax.broadcasted_iota(jnp.int32, (16, SUBS, LANES), 1)
    skew = skew - SUBS * lax.broadcasted_iota(jnp.int32, (16, SUBS, LANES), 0)

    def fill(start, stop, diff_of, keep):
        def body(i, _):
            at = start + i * 16
            limit_ref[pl.ds(at, 16)] = jnp.where(keep(diff_of(at)), -LOW, LOW)
            return 0

        lax.fori_loop(0, (stop - start) // 16, body, 0)

    inside = lambda d: (d > excl) & (d <= band)
    fill(0, far, lambda at: skew + SUBS * (far - at), inside)
    fill(far, 2 * far, lambda at: SUBS * (at - far) - skew, inside)
    fill(2 * far, total, lambda at: skew + SUBS * (base_own - at), lambda d: jnp.abs(d) > excl)

    def base_of(slot, row):
        d_blk, d_plane = PLACE[slot]
        g = at_plane(d_plane) * 2 + core
        mine = plane * 2 + row
        if d_blk == 0:
            step = g - mine
            return jnp.where(step == 0, base_own, far - unit * step)
        if d_blk == 1:
            return far - unit * jnp.where(blk == blocks - 1, 17, groups + g - mine)
        return far + unit * jnp.where(blk == 0, 17, groups + mine - g)

    def is_last(d_blk, d_plane, c):
        return (blk + d_blk == blocks - 1) & (at_plane(d_plane) == planes - 1) & (c == 1)

    def windows(slot, over):
        line = x_ref[slot]
        rest = jnp.where(over, tail_ref[...], line[:, count:])
        return normal_windows(jnp.concatenate([line[:, :count], rest], 1), count, width)

    def piece_windows(slot, over):
        @pl.when(slot != 0)
        def _():
            pieces_in(slot).wait_recv()
            head_in(slot).wait_recv()

        return windows(slot, over)

    def pieces_in(slot):
        return pltpu.make_async_remote_copy(
            src_ref=own_ref, dst_ref=x_ref.at[slot, :, :count], send_sem=send_sem.at[0],
            recv_sem=recv_sem.at[slot], device_id=sibling, device_id_type=MESH,
        )

    def head_in(slot):
        return pltpu.make_async_remote_copy(
            src_ref=own_ref.at[:, :LANES], dst_ref=x_ref.at[slot, :, count:], send_sem=send_sem.at[0],
            recv_sem=head_sem.at[slot], device_id=sibling, device_id_type=MESH,
        )

    pieces_in(PAIRED).wait_recv()

    @pl.when(core == 0)
    def _():
        x_ref[0, :, count:] = x_ref[PAIRED, :, :LANES]
        pltpu.make_async_remote_copy(
            src_ref=own_ref.at[:, :LANES], dst_ref=x_ref.at[PAIRED, :, count:], send_sem=send_sem.at[0],
            recv_sem=head_sem.at[0], device_id=sibling, device_id_type=MESH,
        ).wait_recv()

    @pl.when(core == 1)
    def _():
        x_ref[PAIRED, :, count:] = own_ref[:, :LANES]
        head_in(0).wait_recv()

    for row in range(2):
        slot = jnp.where(core == row, 0, PAIRED)
        put_rows(rows_ref.at[pl.ds(row * count, count)], windows(slot, is_last(0, 0, row)))

    order = (2, 1, 6, 5, 4, 0, 3, 7, 8)
    returns = {2: 3, 1: 4, 6: 1, 5: 2, 4: 0}
    singles = (1 - core, core)
    last_list = [is_last(*PLACE[slot], core) for slot in order]
    base_lists = [[base_of(slot, row) for slot in order] for row in range(2)]
    back_list = [returns.get(slot, -1) for slot in order]
    step_list = [PLACE[slot][0] for slot in order]
    plane_list = [PLACE[slot][1] for slot in order]

    def build(k, ref):
        put_columns(ref, piece_windows(pick(k, order), pick(k, last_list)))

    def back(k, slot, target):
        return pltpu.make_async_remote_copy(
            src_ref=cols_ref.at[k], dst_ref=got_ref.at[slot], send_sem=back_send_sem.at[k],
            recv_sem=back_recv_sem.at[slot], device_id=target, device_id_type=MESH,
        )

    def give_back(k):
        slot = pick(k, back_list)

        @pl.when(slot >= 0)
        def _():
            back(k, slot, device(pick(k, step_list), pick(k, plane_list), core)).start()

    def meet_one(k, now_ref, row):
        base = jnp.where(row == 0, base_lists[0][k], base_lists[1][k])
        cols_ref[k] = tile(rows_ref, now_ref, best_ref, limit_ref, row, base)
        give_back(k)

    def meet(k, now_ref):
        tops = [
            tile(rows_ref, now_ref, best_ref, limit_ref, row, pick(k, base_lists[row]))
            for row in range(2)
        ]
        cols_ref[k] = jnp.maximum(*tops)
        give_back(k)

    build(0, even_ref)
    build(1, odd_ref)
    meet_one(0, even_ref, singles[0])
    build(2, even_ref)
    meet_one(1, odd_ref, singles[1])

    def pair(i, _):
        k = 2 * i + 2
        build(k + 1, odd_ref)
        meet(k, even_ref)
        build(k + 2, even_ref)
        meet(k + 1, odd_ref)
        return 0

    lax.fori_loop(0, 3, pair, 0)
    meet(8, even_ref)

    def row_tops(row):
        return jnp.max(jnp.transpose(best_ref[pl.ds(row * count, count), :]), 0, keepdims=True)

    cols_ref[9] = row_tops(1 - core)
    back(9, 5, sibling).start()
    top = jnp.maximum(row_tops(core), cols_ref[order.index(0)])
    for slot in range(1, 10):
        pieces[slot].wait_send()

    @pl.when(core == 0)
    def _():
        for copy in heads_even.values():
            copy.wait_send()

    @pl.when(core == 1)
    def _():
        for copy in heads_odd.values():
            copy.wait_send()

    for slot, k in enumerate((4, 2, 3, 0, 1, 9)):
        back(k, slot, sibling).wait()
        top = jnp.maximum(top, got_ref[slot])
    out_ref[...] = 1.0 - top * (1.0 / width)


def on_device(blocks, groups, series, tail, excl, band):
    count = series.shape[0]
    width = tail.shape[0] + 1
    hbm = pl.BlockSpec(memory_space=pltpu.HBM)
    window_cols = pltpu.VMEM((4 * width, count), jnp.bfloat16)
    out = pl.pallas_call(
        functools.partial(kernel, blocks, groups, width),
        out_shape=jax.ShapeDtypeStruct((1, count), jnp.float32),
        in_specs=[hbm, hbm, hbm, hbm],
        out_specs=pl.BlockSpec(memory_space=pltpu.VMEM),
        scratch_shapes=[
            pltpu.VMEM((1, count), jnp.float32),
            pltpu.VMEM((1, width - 1), jnp.float32),
            pltpu.VMEM((1, LANES), jnp.float32),
            pltpu.SMEM((1,), jnp.int32),
            pltpu.SMEM((1,), jnp.int32),
            pltpu.VMEM((10, 1, count + LANES), jnp.float32),
            pltpu.VMEM((2 * count, 4 * width), jnp.bfloat16),
            window_cols,
            window_cols,
            pltpu.VMEM((2 * count, LANES), jnp.float32),
            pltpu.VMEM((38 * count // SUBS, SUBS, LANES), jnp.float32),
            pltpu.VMEM((10, 1, count), jnp.float32),
            pltpu.VMEM((6, 1, count), jnp.float32),
            pltpu.SemaphoreType.DMA((4,)),
            pltpu.SemaphoreType.DMA((20,)),
            pltpu.SemaphoreType.DMA((10,)),
            pltpu.SemaphoreType.DMA((10,)),
            pltpu.SemaphoreType.DMA((10,)),
            pltpu.SemaphoreType.DMA((6,)),
            pltpu.SemaphoreType.REGULAR,
        ],
        compiler_params=pltpu.CompilerParams(
            collective_id=0, has_side_effects=True, vmem_limit_bytes=48 * 1024 * 1024
        ),
    )(series.reshape(1, count), tail.reshape(1, width - 1), excl, band)
    return out.reshape(count)


def solution(mesh):
    placed = (P(("blk", "merge")), P(), P(), P())
    body = functools.partial(on_device, mesh.shape["blk"], mesh.shape["merge"])
    return jax.shard_map(
        body, mesh=mesh, in_specs=placed, out_specs=P(("blk", "merge")), check_vma=False
    )
```

time: 49.8 us -> 41.1 us (0.83)
  Pallas kernels: 47.1 us -> 38.3 us
    pallas_call x1, Pallas kernels: 47.1 us -> 38.3 us  [on_device(): pl.pallas_call(functools.partial(kernel, blocks, groups, width), out_shap...]
where the time goes in v2:
time: 41.1 us; the launch traced here: 40.8 us
  Pallas kernels  38.3 us (93%)
  between operations  1.34 us (3%)
  local copies, waits for them, and re-layouts  1.24 us (3%)
    pallas_call x1, Pallas kernels, on_device(): pl.pallas_call(functools.partial(kernel, blocks, groups, width), out_shap...  38.3 us
    unnamed x5, local copies, waits for them, and re-layouts  1.24 us

profile of v2, /device:TPU:1, one launch (start us, length us, event | category | flops | bytes accessed | tf_op | source)
XLA Modules:
  0.0 40.8 jit_solution(18099449889975025874)
XLA Ops:
  0.0 0.0 copy-start
  1.3 0.0 copy-start.1
  1.3 0.0 copy-done
  1.3 0.6 %copy-done.1 = f32[63]{0:T(128)S(1)} copy-done((f32[63]{0:T(128)S(1)}, f32[63]{0:T(128)}, u32[]{:S(2)}) %copy-start.1) | copy-done | bytes 276
  2.0 38.3 %shard_map.46 = f32[1,1024]{1,0:T(1,128)S(1)} custom-call(f32[1,1024]{1,0:T(1,128)S(1)} %bitcast.4, f32[1,63]{1,0:T(1,128)S(1)} %bitcast.5, s32[1]{0:T(128)S(6)} %copy.6.excl_hbm, s32[1]{0:T(128)S(6)} %copy.7.band_hbm), custom_call_target="tpu_custom_call" | custom-call | tf_op jit(solution)/shard_map/pallas_call | solution.py:357
  40.2 0.6 %copy.8 = f32[1024]{0:T(1024)} copy(f32[1024]{0:T(1024)S(1)} %bitcast.3) | data formatting | bytes 8192
Async XLA Ops:
  0.0 1.3 %copy-start = (f32[1024]{0:T(1024)S(1)}, f32[1024]{0:T(1024)}, u32[]{:S(2)}) copy-start(f32[1024]{0:T(1024)} %param.4) | copy-start | bytes 12292
  1.3 0.7 %copy-start.1 = (f32[63]{0:T(128)S(1)}, f32[63]{0:T(128)}, u32[]{:S(2)}) copy-start(f32[63]{0:T(128)} %param.5) | copy-start | bytes 760

commit v3 on v2

--- a/solution.py
+++ b/solution.py
@@ -84,7 +84,7 @@
     blocks, groups, width,
     series_hbm, tail_hbm, excl_hbm, band_hbm, out_ref,
     own_ref, short_ref, tail_ref, excl_ref, band_ref, x_ref, rows_ref, even_ref, odd_ref, best_ref, limit_ref,
-    cols_ref, got_ref, local_sem, send_sem, recv_sem, head_sem, back_send_sem, back_recv_sem, ready_sem,
+    cols_ref, got_ref, local_sem, send_sem, recv_sem, head_sem, back_send_sem, back_recv_sem, ready_sem, far_sem,
 ):
     count = own_ref.shape[1]
     unit = count // SUBS
@@ -115,27 +115,78 @@
     def greet(target):
         pl.semaphore_signal(barrier, inc=1, device_id=target, device_id_type=MESH)
 
-    for d_blk in (0, 1, -1):
-        greet(device(d_blk, 2, 0))
+    ahead = plane < 2
+
+    @pl.when(ahead)
+    def _():
+        for d_blk in (0, 1, -1):
+            greet(device(d_blk, 2, 0))
+
     greet(sibling)
     for d_blk, d_plane in ((0, 1), (0, -1), (1, 0), (1, 1), (1, -1)):
         greet(device(d_blk, d_plane, 1))
 
     @pl.when(core == 1)
     def _():
-        greet((lax.rem(blk + 2, blocks), jnp.where(plane == 2, 0, 1)))
+        @pl.when(plane != 2)
+        def _():
+            greet((lax.rem(blk + 2, blocks), 1))
 
         @pl.when(plane != 1)
         def _():
             greet(device(-1, -1, 1))
 
-    loads[0].wait()
+    far = 18 * unit
+    base_own = 37 * unit
+    total = 38 * unit
+
+    def fill_bounds():
+        excl = excl_ref[0]
+        band = band_ref[0]
+        skew = lax.broadcasted_iota(jnp.int32, (16, SUBS, LANES), 2)
+        skew = skew - lax.broadcasted_iota(jnp.int32, (16, SUBS, LANES), 1)
+        skew = skew - SUBS * lax.broadcasted_iota(jnp.int32, (16, SUBS, LANES), 0)
+
+        def fill(start, stop, diff_of, keep):
+            def body(i, _):
+                at = start + i * 16
+                limit_ref[pl.ds(at, 16)] = jnp.where(keep(diff_of(at)), -LOW, LOW)
+                return 0
+
+            lax.fori_loop(0, (stop - start) // 16, body, 0)
+
+        inside = lambda d: (d > excl) & (d <= band)
+        fill(0, far, lambda at: skew + SUBS * (far - at), inside)
+        fill(far, 2 * far, lambda at: SUBS * (at - far) - skew, inside)
+        fill(2 * far, total, lambda at: skew + SUBS * (base_own - at), lambda d: jnp.abs(d) > excl)
+
+    for load in loads:
+        load.wait()
     x_ref[0, :, :count] = own_ref[...]
+
+    @pl.when(ahead)
+    def _():
+        fill_bounds()
+
     first_plane = plane == 0
-    far_count = 7 + jnp.where(first_plane, 1, 0)
+    far_count = jnp.where(ahead, 1, 7)
     near_count = 11 + jnp.where(first_plane, 3, 1)
     pl.semaphore_wait(barrier, jnp.where(core == 0, far_count, near_count))
-    pl.semaphore_signal(ready_sem, inc=1, device_id=sibling, device_id_type=MESH)
+
+    def tell(sem, target):
+        pl.semaphore_signal(sem, inc=1, device_id=target, device_id_type=MESH)
+
+    behind = jnp.logical_not(ahead)
+
+    @pl.when((core == 1) | behind)
+    def _():
+        tell(ready_sem, sibling)
+
+    @pl.when((core == 0) & behind)
+    def _():
+        for d_blk in (0, 1, -1):
+            tell(far_sem, device(d_blk, 2, 0))
+
 
     def send_piece(slot, target):
         return pltpu.make_async_remote_copy(
@@ -153,29 +204,46 @@
     pieces = {slot: send_piece(slot, device(d, dp, core)) for d, dp, slot in SPREAD}
     pieces[PAIRED] = send_piece(PAIRED, sibling)
     heads_odd = {slot: send_head(slot, slot, device(d, dp, 0)) for d, dp, slot in SPREAD}
-    heads_even = {slot: send_head(slot, slot, device(back_blk + d, dp - 1, 1)) for d, dp, slot in SPREAD}
+    heads_even = {
+        slot: send_head(slot, slot, device(back_blk + d, dp - 1, 1)) for d, dp, slot in SPREAD if dp != -1
+    }
     heads_even[0] = send_head(0, 0, device(back_blk, -1, 1))
     heads_even[9] = send_head(PAIRED, 9, device(back_blk, -1, 0))
 
-    @pl.when(core == 0)
-    def _():
+    def far_even():
         for slot in (3, 7, 8):
             pieces[slot].start()
-        for slot in (1, 5):
+
+    def near_even():
+        pl.semaphore_wait(ready_sem, 1)
+        for slot in (0, 9):
             heads_even[slot].start()
-        pl.semaphore_wait(ready_sem, 1)
         pieces[PAIRED].start()
-        for slot in (0, 9, 2, 3, 4, 6, 7, 8):
+        for slot in (2, 6):
+            pieces[slot].start()
             heads_even[slot].start()
-        for slot in (1, 2, 5, 6, 4):
+        for slot in (4, 5, 1):
             pieces[slot].start()
+        for slot in (4, 3, 7, 8):
+            heads_even[slot].start()
+
+    @pl.when((core == 0) & behind)
+    def _():
+        far_even()
+        near_even()
+
+    @pl.when((core == 0) & ahead)
+    def _():
+        near_even()
+        pl.semaphore_wait(far_sem, 3)
+        tell(ready_sem, sibling)
+        far_even()
 
     @pl.when(core == 1)
     def _():
         pieces[PAIRED].start()
-        for slot in (1, 2, 5, 6, 4):
+        for slot in (2, 6, 4, 5, 1):
             pieces[slot].start()
-        for slot in (1, 2, 5, 6, 4):
             heads_odd[slot].start()
         pl.semaphore_wait(ready_sem, 1)
         for slot in (3, 7, 8):
@@ -183,33 +251,13 @@
         for slot in (3, 7, 8):
             heads_odd[slot].start()
 
-    for load in loads[1:]:
-        load.wait()
     tail_ref[...] = jnp.zeros(tail_ref.shape, jnp.float32)
     tail_ref[:, : width - 1] = short_ref[...]
     best_ref[...] = jnp.full(best_ref.shape, LOW, jnp.float32)
 
-    far = 18 * unit
-    base_own = 37 * unit
-    total = 38 * unit
-    excl = excl_ref[0]
-    band = band_ref[0]
-    skew = lax.broadcasted_iota(jnp.int32, (16, SUBS, LANES), 2)
-    skew = skew - lax.broadcasted_iota(jnp.int32, (16, SUBS, LANES), 1)
-    skew = skew - SUBS * lax.broadcasted_iota(jnp.int32, (16, SUBS, LANES), 0)
-
-    def fill(start, stop, diff_of, keep):
-        def body(i, _):
-            at = start + i * 16
-            limit_ref[pl.ds(at, 16)] = jnp.where(keep(diff_of(at)), -LOW, LOW)
-            return 0
-
-        lax.fori_loop(0, (stop - start) // 16, body, 0)
-
-    inside = lambda d: (d > excl) & (d <= band)
-    fill(0, far, lambda at: skew + SUBS * (far - at), inside)
-    fill(far, 2 * far, lambda at: SUBS * (at - far) - skew, inside)
-    fill(2 * far, total, lambda at: skew + SUBS * (base_own - at), lambda d: jnp.abs(d) > excl)
+    @pl.when(behind)
+    def _():
+        fill_bounds()
 
     def base_of(slot, row):
         d_blk, d_plane = PLACE[slot]
@@ -230,14 +278,6 @@
         rest = jnp.where(over, tail_ref[...], line[:, count:])
         return normal_windows(jnp.concatenate([line[:, :count], rest], 1), count, width)
 
-    def piece_windows(slot, over):
-        @pl.when(slot != 0)
-        def _():
-            pieces_in(slot).wait_recv()
-            head_in(slot).wait_recv()
-
-        return windows(slot, over)
-
     def pieces_in(slot):
         return pltpu.make_async_remote_copy(
             src_ref=own_ref, dst_ref=x_ref.at[slot, :, :count], send_sem=send_sem.at[0],
@@ -249,6 +289,14 @@
             src_ref=own_ref.at[:, :LANES], dst_ref=x_ref.at[slot, :, count:], send_sem=send_sem.at[0],
             recv_sem=head_sem.at[slot], device_id=sibling, device_id_type=MESH,
         )
+
+    relays = [
+        pltpu.make_async_remote_copy(
+            src_ref=x_ref.at[0, :, count:], dst_ref=x_ref.at[slot, :, count:], send_sem=send_sem.at[20 + at],
+            recv_sem=head_sem.at[slot], device_id=device(-at, -1, 1), device_id_type=MESH,
+        )
+        for at, slot in enumerate((1, 5))
+    ]
 
     pieces_in(PAIRED).wait_recv()
 
@@ -264,72 +312,116 @@
     def _():
         x_ref[PAIRED, :, count:] = own_ref[:, :LANES]
         head_in(0).wait_recv()
+        for copy in relays:
+            copy.start()
 
     for row in range(2):
         slot = jnp.where(core == row, 0, PAIRED)
         put_rows(rows_ref.at[pl.ds(row * count, count)], windows(slot, is_last(0, 0, row)))
 
-    order = (2, 1, 6, 5, 4, 0, 3, 7, 8)
-    returns = {2: 3, 1: 4, 6: 1, 5: 2, 4: 0}
-    singles = (1 - core, core)
-    last_list = [is_last(*PLACE[slot], core) for slot in order]
-    base_lists = [[base_of(slot, row) for slot in order] for row in range(2)]
-    back_list = [returns.get(slot, -1) for slot in order]
-    step_list = [PLACE[slot][0] for slot in order]
-    plane_list = [PLACE[slot][1] for slot in order]
-
-    def build(k, ref):
-        put_columns(ref, piece_windows(pick(k, order), pick(k, last_list)))
-
-    def back(k, slot, target):
+    slots = len(PLACE)
+    last_plane = plane == planes - 1
+    shared = (jnp.where(last_plane, 1, 2), jnp.where(last_plane, 2, 1))
+    common = (4, 0, 3, 7, 8)
+    order = [
+        jnp.where(first_plane, at_first, jnp.where(last_plane, at_last, between))
+        for at_first, at_last, between in zip((6, 4, 0, 5) + common[2:], (5, 6) + common, (6, 5) + common)
+    ]
+    last_list = [is_last(*PLACE[slot], core) for slot in range(slots)]
+    base_lists = [[base_of(slot, row) for slot in range(slots)] for row in range(2)]
+    step_list = [PLACE[slot][0] for slot in range(slots)]
+    plane_list = [PLACE[slot][1] for slot in range(slots)]
+    back_list = [-1, 4, 3, -1, 0, 2, 1, -1, -1]
+
+    def build(slot, ref):
+        put_columns(ref, windows(slot, pick(slot, last_list)))
+
+    def arrive(slot):
+        @pl.when(slot != 0)
+        def _():
+            pieces_in(slot).wait_recv()
+            head_in(slot).wait_recv()
+
+    def back(slot, at, target):
         return pltpu.make_async_remote_copy(
-            src_ref=cols_ref.at[k], dst_ref=got_ref.at[slot], send_sem=back_send_sem.at[k],
-            recv_sem=back_recv_sem.at[slot], device_id=target, device_id_type=MESH,
-        )
-
-    def give_back(k):
-        slot = pick(k, back_list)
-
-        @pl.when(slot >= 0)
-        def _():
-            back(k, slot, device(pick(k, step_list), pick(k, plane_list), core)).start()
-
-    def meet_one(k, now_ref, row):
-        base = jnp.where(row == 0, base_lists[0][k], base_lists[1][k])
-        cols_ref[k] = tile(rows_ref, now_ref, best_ref, limit_ref, row, base)
-        give_back(k)
-
-    def meet(k, now_ref):
+            src_ref=cols_ref.at[slot], dst_ref=got_ref.at[at], send_sem=back_send_sem.at[slot],
+            recv_sem=back_recv_sem.at[at], device_id=target, device_id_type=MESH,
+        )
+
+    def give_back(slot):
+        back(slot, pick(slot, back_list), device(pick(slot, step_list), pick(slot, plane_list), core)).start()
+
+    def meet_shared(slot, now_ref):
+        one = jnp.where(slot == 2, 1 - core, core)
+        whole = plane == jnp.where(slot == 2, 1, planes - 1)
+        low = jnp.where(whole, 0, one)
+        high = jnp.where(whole, 2, jnp.where(first_plane, one, one + 1))
+        cols_ref[slot] = jnp.full((1, count), LOW, jnp.float32)
+
+        def body(at, _):
+            base = jnp.where(at == 0, pick(slot, base_lists[0]), pick(slot, base_lists[1]))
+            top = tile(rows_ref, now_ref, best_ref, limit_ref, at, base)
+            cols_ref[slot] = jnp.maximum(cols_ref[slot], top)
+            return 0
+
+        lax.fori_loop(low, high, body, 0)
+
+        @pl.when(plane != 0)
+        def _():
+            give_back(slot)
+
+    def meet(slot, now_ref):
         tops = [
-            tile(rows_ref, now_ref, best_ref, limit_ref, row, pick(k, base_lists[row]))
+            tile(rows_ref, now_ref, best_ref, limit_ref, row, pick(slot, base_lists[row]))
             for row in range(2)
         ]
-        cols_ref[k] = jnp.maximum(*tops)
-        give_back(k)
-
-    build(0, even_ref)
-    build(1, odd_ref)
-    meet_one(0, even_ref, singles[0])
-    build(2, even_ref)
-    meet_one(1, odd_ref, singles[1])
+        cols_ref[slot] = jnp.maximum(*tops)
+
+        @pl.when(pick(slot, back_list) >= 0)
+        def _():
+            give_back(slot)
+
+    @pl.when(plane != 0)
+    def _():
+        arrive(shared[0])
+        build(shared[0], even_ref)
+
+    meet_shared(shared[0], even_ref)
+    arrive(order[0])
+    build(order[0], odd_ref)
+
+    @pl.when(plane != 0)
+    def _():
+        arrive(shared[1])
+        build(shared[1], even_ref)
+
+    meet_shared(shared[1], even_ref)
 
     def pair(i, _):
-        k = 2 * i + 2
-        build(k + 1, odd_ref)
-        meet(k, even_ref)
-        build(k + 2, even_ref)
-        meet(k + 1, odd_ref)
+        k = 2 * i
+        now, then, after = (pick(k + at, order) for at in range(3))
+        arrive(then)
+        build(then, even_ref)
+        meet(now, odd_ref)
+        arrive(after)
+        build(after, odd_ref)
+        meet(then, even_ref)
         return 0
 
     lax.fori_loop(0, 3, pair, 0)
-    meet(8, even_ref)
+    meet(order[6], odd_ref)
+
+    @pl.when(plane == 0)
+    def _():
+        for slot in (1, 2):
+            arrive(slot)
 
     def row_tops(row):
         return jnp.max(jnp.transpose(best_ref[pl.ds(row * count, count), :]), 0, keepdims=True)
 
     cols_ref[9] = row_tops(1 - core)
     back(9, 5, sibling).start()
-    top = jnp.maximum(row_tops(core), cols_ref[order.index(0)])
+    top = jnp.maximum(row_tops(core), cols_ref[0])
     for slot in range(1, 10):
         pieces[slot].wait_send()
 
@@ -340,11 +432,30 @@
 
     @pl.when(core == 1)
     def _():
-        for copy in heads_odd.values():
+        for copy in list(heads_odd.values()) + relays:
             copy.wait_send()
 
-    for slot, k in enumerate((4, 2, 3, 0, 1, 9)):
-        back(k, slot, sibling).wait()
+    for slot in (4, 5, 6, 9):
+        back(slot, 0, sibling).wait_send()
+
+    @pl.when(plane != 0)
+    def _():
+        for slot in (1, 2):
+            back(slot, 0, sibling).wait_send()
+
+    for slot, silent in ((3, planes - 1), (4, 1)):
+
+        @pl.when(plane == silent)
+        def _():
+            got_ref[slot] = jnp.full((1, count), LOW, jnp.float32)
+
+        @pl.when(plane != silent)
+        def _():
+            back(0, slot, sibling).wait_recv()
+
+    for slot in (0, 1, 2, 5):
+        back(0, slot, sibling).wait_recv()
+    for slot in range(6):
         top = jnp.maximum(top, got_ref[slot])
     out_ref[...] = 1.0 - top * (1.0 / width)
 
@@ -374,17 +485,18 @@
             pltpu.VMEM((10, 1, count), jnp.float32),
             pltpu.VMEM((6, 1, count), jnp.float32),
             pltpu.SemaphoreType.DMA((4,)),
-            pltpu.SemaphoreType.DMA((20,)),
+            pltpu.SemaphoreType.DMA((22,)),
             pltpu.SemaphoreType.DMA((10,)),
             pltpu.SemaphoreType.DMA((10,)),
             pltpu.SemaphoreType.DMA((10,)),
             pltpu.SemaphoreType.DMA((6,)),
             pltpu.SemaphoreType.REGULAR,
+            pltpu.SemaphoreType.REGULAR,
         ],
         compiler_params=pltpu.CompilerParams(
             collective_id=0, has_side_effects=True, vmem_limit_bytes=48 * 1024 * 1024
         ),
-    )(series.reshape(1, count), tail.reshape(1, width - 1), excl, band)
+    )(series.reshape(1, count), pltpu.with_memory_space_constraint(tail.reshape(1, width - 1), pltpu.HBM), excl, band)
     return out.reshape(count)
 
 

time: 41.1 us -> 39.3 us (0.956)
  Pallas kernels: 38.3 us -> 37.2 us
  local copies, waits for them, and re-layouts: 1.24 us -> 0.6 us
    pallas_call x1, Pallas kernels: 38.3 us -> 37.2 us  [on_device(): pl.pallas_call(functools.partial(kernel, blocks, groups, width), out_shap...]
    unnamed x5 -> x3, local copies, waits for them, and re-layouts: 1.24 us -> 0.6 us
where the time goes in v3:
time: 39.3 us; the launch traced here: 39.2 us
  Pallas kernels  37.2 us (95%)
  between operations  1.33 us (3%)
  local copies, waits for them, and re-layouts  0.6 us (2%)
    pallas_call x1, Pallas kernels, on_device(): pl.pallas_call(functools.partial(kernel, blocks, groups, width), out_shap...  37.2 us

profile of v3, /device:TPU:1, one launch (start us, length us, event | category | flops | bytes accessed | tf_op | source)
XLA Modules:
  0.0 39.2 jit_solution(1281546950078695531)
XLA Ops:
  0.0 0.0 copy-start
  1.3 0.0 copy-done
  1.3 37.2 %shard_map.46 = f32[1,1024]{1,0:T(1,128)S(1)} custom-call(f32[1,1024]{1,0:T(1,128)S(1)} %bitcast.4, f32[1,63]{1,0:T(1,128)} %bitcast.5, s32[1]{0:T(128)S(6)} %copy.6.excl_hbm, s32[1]{0:T(128)S(6)} %copy.7.band_hbm), custom_call_target="tpu_custom_call" | custom-call | tf_op jit(solution)/shard_map/pallas_call | solution.py:468
  38.6 0.6 %copy.8 = f32[1024]{0:T(1024)} copy(f32[1024]{0:T(1024)S(1)} %bitcast.3) | data formatting | bytes 8192
Async XLA Ops:
  0.0 1.3 %copy-start = (f32[1024]{0:T(1024)S(1)}, f32[1024]{0:T(1024)}, u32[]{:S(2)}) copy-start(f32[1024]{0:T(1024)} %param.4) | copy-start | bytes 12292

commit v4 on v3

--- a/solution.py
+++ b/solution.py
@@ -327,6 +327,9 @@
         jnp.where(first_plane, at_first, jnp.where(last_plane, at_last, between))
         for at_first, at_last, between in zip((6, 4, 0, 5) + common[2:], (5, 6) + common, (6, 5) + common)
     ]
+    opens = blk == 0
+    closes = blk == blocks - 1
+    order[6] = jnp.where(opens, 0, 8)
     last_list = [is_last(*PLACE[slot], core) for slot in range(slots)]
     base_lists = [[base_of(slot, row) for slot in range(slots)] for row in range(2)]
     step_list = [PLACE[slot][0] for slot in range(slots)]
@@ -377,7 +380,9 @@
         ]
         cols_ref[slot] = jnp.maximum(*tops)
 
-        @pl.when(pick(slot, back_list) >= 0)
+        beyond = closes & (pick(slot, step_list) == 1)
+
+        @pl.when((pick(slot, back_list) >= 0) & jnp.logical_not(beyond))
         def _():
             give_back(slot)
 
@@ -409,7 +414,17 @@
         return 0
 
     lax.fori_loop(0, 3, pair, 0)
-    meet(order[6], odd_ref)
+    def meet_last(row):
+        @pl.when(jnp.logical_not(opens))
+        def _():
+            base = jnp.where(row == 0, base_lists[0][8], base_lists[1][8])
+            tile(rows_ref, odd_ref, best_ref, limit_ref, row, base)
+
+    @pl.when(opens)
+    def _():
+        arrive(8)
+
+    meet_last(1 - core)
 
     @pl.when(plane == 0)
     def _():
@@ -421,6 +436,7 @@
 
     cols_ref[9] = row_tops(1 - core)
     back(9, 5, sibling).start()
+    meet_last(core)
     top = jnp.maximum(row_tops(core), cols_ref[0])
     for slot in range(1, 10):
         pieces[slot].wait_send()
@@ -435,8 +451,12 @@
         for copy in list(heads_odd.values()) + relays:
             copy.wait_send()
 
-    for slot in (4, 5, 6, 9):
-        back(slot, 0, sibling).wait_send()
+    back(9, 0, sibling).wait_send()
+
+    @pl.when(jnp.logical_not(closes))
+    def _():
+        for slot in (4, 5, 6):
+            back(slot, 0, sibling).wait_send()
 
     @pl.when(plane != 0)
     def _():
@@ -453,8 +473,18 @@
         def _():
             back(0, slot, sibling).wait_recv()
 
-    for slot in (0, 1, 2, 5):
-        back(0, slot, sibling).wait_recv()
+    back(0, 5, sibling).wait_recv()
+
+    @pl.when(opens)
+    def _():
+        for slot in range(3):
+            got_ref[slot] = jnp.full((1, count), LOW, jnp.float32)
+
+    @pl.when(jnp.logical_not(opens))
+    def _():
+        for slot in range(3):
+            back(0, slot, sibling).wait_recv()
+
     for slot in range(6):
         top = jnp.maximum(top, got_ref[slot])
     out_ref[...] = 1.0 - top * (1.0 / width)

time: 39.3 us -> 38.5 us (0.980)
  the two profiles are of different devices: /device:TPU:1 before, /device:TPU:33 now
where the time goes in v4:
time: 38.5 us; the launch traced here: 38.4 us
  Pallas kernels  36.4 us (95%)
  between operations  1.33 us (3%)
  local copies, waits for them, and re-layouts  0.6 us (2%)
    pallas_call x1, Pallas kernels, on_device(): pl.pallas_call(functools.partial(kernel, blocks, groups, width), out_shap...  36.4 us

profile of v4, /device:TPU:33, one launch (start us, length us, event | category | flops | bytes accessed | tf_op | source)
XLA Modules:
  0.0 38.4 jit_solution(12495942053627611294)
XLA Ops:
  0.0 0.0 copy-start
  1.3 0.0 copy-done
  1.3 36.4 %shard_map.46 = f32[1,1024]{1,0:T(1,128)S(1)} custom-call(f32[1,1024]{1,0:T(1,128)S(1)} %bitcast.4, f32[1,63]{1,0:T(1,128)} %bitcast.5, s32[1]{0:T(128)S(6)} %copy.6.excl_hbm, s32[1]{0:T(128)S(6)} %copy.7.band_hbm), custom_call_target="tpu_custom_call" | custom-call | tf_op jit(solution)/shard_map/pallas_call | solution.py:498
  37.8 0.6 %copy.8 = f32[1024]{0:T(1024)} copy(f32[1024]{0:T(1024)S(1)} %bitcast.3) | data formatting | bytes 8192
Async XLA Ops:
  0.0 1.3 %copy-start = (f32[1024]{0:T(1024)S(1)}, f32[1024]{0:T(1024)}, u32[]{:S(2)}) copy-start(f32[1024]{0:T(1024)} %param.4) | copy-start | bytes 12292

commit v5 on v4

--- a/solution.py
+++ b/solution.py
@@ -386,14 +386,18 @@
         def _():
             give_back(slot)
 
+    arrive(order[0])
+    build(order[0], odd_ref)
+
     @pl.when(plane != 0)
     def _():
         arrive(shared[0])
         build(shared[0], even_ref)
 
+    meet(order[0], odd_ref)
+    arrive(order[1])
+    build(order[1], odd_ref)
     meet_shared(shared[0], even_ref)
-    arrive(order[0])
-    build(order[0], odd_ref)
 
     @pl.when(plane != 0)
     def _():
@@ -403,7 +407,7 @@
     meet_shared(shared[1], even_ref)
 
     def pair(i, _):
-        k = 2 * i
+        k = 2 * i + 1
         now, then, after = (pick(k + at, order) for at in range(3))
         arrive(then)
         build(then, even_ref)
@@ -413,12 +417,16 @@
         meet(then, even_ref)
         return 0
 
-    lax.fori_loop(0, 3, pair, 0)
+    lax.fori_loop(0, 2, pair, 0)
+    arrive(order[6])
+    build(order[6], even_ref)
+    meet(order[5], odd_ref)
+
     def meet_last(row):
         @pl.when(jnp.logical_not(opens))
         def _():
             base = jnp.where(row == 0, base_lists[0][8], base_lists[1][8])
-            tile(rows_ref, odd_ref, best_ref, limit_ref, row, base)
+            tile(rows_ref, even_ref, best_ref, limit_ref, row, base)
 
     @pl.when(opens)
     def _():

time: 38.5 us -> 37.8 us (0.982)
  the two profiles are of different devices: /device:TPU:33 before, /device:TPU:1 now
where the time goes in v5:
time: 37.8 us; the launch traced here: 37.6 us
  Pallas kernels  35.7 us (94%)
  between operations  1.33 us (4%)
  local copies, waits for them, and re-layouts  0.6 us (2%)
    pallas_call x1, Pallas kernels, on_device(): pl.pallas_call(functools.partial(kernel, blocks, groups, width), out_shap...  35.7 us

profile of v5, /device:TPU:1, one launch (start us, length us, event | category | flops | bytes accessed | tf_op | source)
XLA Modules:
  0.0 37.6 jit_solution(9490786002346729957)
XLA Ops:
  0.0 0.0 copy-start
  1.3 0.0 copy-done
  1.3 35.7 %shard_map.46 = f32[1,1024]{1,0:T(1,128)S(1)} custom-call(f32[1,1024]{1,0:T(1,128)S(1)} %bitcast.4, f32[1,63]{1,0:T(1,128)} %bitcast.5, s32[1]{0:T(128)S(6)} %copy.6.excl_hbm, s32[1]{0:T(128)S(6)} %copy.7.band_hbm), custom_call_target="tpu_custom_call" | custom-call | tf_op jit(solution)/shard_map/pallas_call | solution.py:506
  37.0 0.6 %copy.8 = f32[1024]{0:T(1024)} copy(f32[1024]{0:T(1024)S(1)} %bitcast.3) | data formatting | bytes 8192
Async XLA Ops:
  0.0 1.3 %copy-start = (f32[1024]{0:T(1024)S(1)}, f32[1024]{0:T(1024)}, u32[]{:S(2)}) copy-start(f32[1024]{0:T(1024)} %param.4) | copy-start | bytes 12292

commit v6 on v5

--- a/solution.py
+++ b/solution.py
@@ -325,7 +325,7 @@
     common = (4, 0, 3, 7, 8)
     order = [
         jnp.where(first_plane, at_first, jnp.where(last_plane, at_last, between))
-        for at_first, at_last, between in zip((6, 4, 0, 5) + common[2:], (5, 6) + common, (6, 5) + common)
+        for at_first, at_last, between in zip((4, 6, 0, 5) + common[2:], (5, 6) + common, (6, 5) + common)
     ]
     opens = blk == 0
     closes = blk == blocks - 1

time: 37.8 us -> 37.8 us (level)
  no operation moved by 1% of the time
where the time goes in v6:
time: 37.8 us; the launch traced here: 37.6 us
  Pallas kernels  35.7 us (94%)
  between operations  1.33 us (4%)
  local copies, waits for them, and re-layouts  0.6 us (2%)
    pallas_call x1, Pallas kernels, on_device(): pl.pallas_call(functools.partial(kernel, blocks, groups, width), out_shap...  35.7 us

profile of v6, /device:TPU:1, one launch (start us, length us, event | category | flops | bytes accessed | tf_op | source)
XLA Modules:
  0.0 37.6 jit_solution(11990934300056915623)
XLA Ops:
  0.0 0.0 copy-start
  1.3 0.0 copy-done
  1.3 35.7 %shard_map.46 = f32[1,1024]{1,0:T(1,128)S(1)} custom-call(f32[1,1024]{1,0:T(1,128)S(1)} %bitcast.4, f32[1,63]{1,0:T(1,128)} %bitcast.5, s32[1]{0:T(128)S(6)} %copy.6.excl_hbm, s32[1]{0:T(128)S(6)} %copy.7.band_hbm), custom_call_target="tpu_custom_call" | custom-call | tf_op jit(solution)/shard_map/pallas_call | solution.py:506
  37.0 0.6 %copy.8 = f32[1024]{0:T(1024)} copy(f32[1024]{0:T(1024)S(1)} %bitcast.3) | data formatting | bytes 8192
Async XLA Ops:
  0.0 1.3 %copy-start = (f32[1024]{0:T(1024)S(1)}, f32[1024]{0:T(1024)}, u32[]{:S(2)}) copy-start(f32[1024]{0:T(1024)} %param.4) | copy-start | bytes 12292
